TPU v7x, 32 devices: a whole 2x2x4 slice. The times are simulated.
32 devices in a mesh: seq: 2 (over y), ctx: 4 (over x, core), wt: 4 (over z).
Axes of the slice: x: 2, y: 2, z: 4, core: 2. Of those that a mesh axis runs over, the one named last changes fastest.
Arguments:
- tokens: bfloat16 [16, 1024, 768], P(('seq', 'wt'), 'ctx'), may hold values from -6 to 6
- cotangent: bfloat16 [16, 1024, 768], P(('seq', 'wt'), 'ctx'), may hold values from -6 to 6
- segment_ids: int32 [16, 1024], P(('seq', 'wt'), 'ctx'), may hold values from 0 to 4, as said below
- lengths: int32 [16, 4], P(('seq', 'wt')), may hold values from 32 to 928, as said below
- w_query: bfloat16 [768, 768], P('wt'), may hold values from -0.21875 to 0.21875
- b_query: bfloat16 [768], P('wt'), may hold values from -3 to 3
- w_key: bfloat16 [768, 768], P('wt'), may hold values from -0.21875 to 0.21875
- w_value: bfloat16 [768, 768], P('wt'), may hold values from -0.21875 to 0.21875
- b_value: bfloat16 [768], P('wt'), may hold values from -3 to 3
- w_attn: bfloat16 [768, 768], P('wt'), may hold values from -1.75 to 1.75
- b_attn: bfloat16 [768], P('wt'), may hold values from -2 to 2
- ln1_gain: bfloat16 [768], P('wt'), may hold values from 0.5 to 1.5
- ln1_shift: bfloat16 [768], P('wt'), may hold values from -2 to 2
- w_inner: bfloat16 [768, 3072], P('wt'), may hold values from -0.21875 to 0.21875
- b_inner: bfloat16 [3072], P('wt'), may hold values from -3 to 3
- w_outer: bfloat16 [3072, 768], P('wt'), may hold values from -0.109375 to 0.109375
- b_outer: bfloat16 [768], P('wt'), may hold values from -2 to 2
- ln2_gain: bfloat16 [768], P('wt'), may hold values from 0.5 to 1.5
- ln2_shift: bfloat16 [768], P('wt'), may hold values from -2 to 2
Outputs:
- layer_out: bfloat16 [16, 1024, 768], P(('seq', 'wt'), 'ctx')
- grad_input: bfloat16 [16, 1024, 768], P(('seq', 'wt'), 'ctx')
- grad_w_query: float32 [768, 768], P('wt')
- grad_b_query: float32 [768], P('wt')
- grad_w_key: float32 [768, 768], P('wt')
- grad_w_value: float32 [768, 768], P('wt')
- grad_b_value: float32 [768], P('wt')
- grad_w_attn: float32 [768, 768], P('wt')
- grad_b_attn: float32 [768], P('wt')
- grad_ln1_gain: float32 [768], P('wt')
- grad_ln1_shift: float32 [768], P('wt')
- grad_w_inner: float32 [768, 3072], P('wt')
- grad_b_inner: float32 [3072], P('wt')
- grad_w_outer: float32 [3072, 768], P('wt')
- grad_b_outer: float32 [768], P('wt')
- grad_ln2_gain: float32 [768], P('wt')
- grad_ln2_shift: float32 [768], P('wt')
Inputs may be any that keep to these rules, and one draw needn't show every extreme that they name: `lengths`: the 4 documents of a sequence lie end to end from its first position, and the positions after them are padding; among the 2 sequences that one device holds, one has a single document of 1024 - 3 * max(1, 32) positions, at a place among its documents that varies, and its other documents have max(1, 32) positions each; every other sequence has documents of 64 to 256 positions. `segment_ids`: position t holds d + 1 where it lies in the sequence's document d (counted from 0 in the order of lengths), and 0 in the padding.
All inputs are finite; a program needn't handle non-finite values.
Results may differ from a plain program's by a relative error of at most 0.02.
Values may be sent and summed in bfloat16 or wider, within the bound.
No kernel may reach another device: no remote copies, remote signals or barrier semaphores. Data moves between devices by JAX's collectives and lax.ppermute only.
A program may use at most 320 MiB of HBM per device.

v0:
```python
import math
import jax
import jax.numpy as jnp
from jax import lax
from jax.sharding import PartitionSpec as P

H = 12
HD = 64
NEG = -1000000000.0
EPS = 1e-05


def product(former, latter):
    return jnp.dot(former, latter, preferred_element_type=jnp.float32)


def over_rows(former, latter):
    return lax.dot_general(
        former, latter, (((0,), (0,)), ((), ())), preferred_element_type=jnp.float32
    )


def against(former, latter):
    return lax.dot_general(
        former, latter, (((1,), (1,)), ((), ())), preferred_element_type=jnp.float32
    )


def norm_rows(values, gain, shift):
    center = jnp.mean(values, axis=-1, keepdims=True)
    offset = values - center
    spread = jnp.mean(offset * offset, axis=-1, keepdims=True)
    return offset * lax.rsqrt(spread + EPS) * gain + shift


def exact_gelu(values):
    return jax.nn.gelu(values, approximate=False)


def key_segments(doc_lens, length):
    doc_ends = jnp.cumsum(doc_lens, axis=-1)
    places = jnp.arange(length, dtype=jnp.int32)
    passed = jnp.sum((places[None, :, None] >= doc_ends[:, None, :]).astype(jnp.int32), axis=-1)
    return jnp.where(places[None, :] < doc_ends[:, -1:], passed + 1, 0)


def to_items(matrix, groups):
    seq_count, length, model_width = matrix.shape
    per_group = model_width // (groups * HD)
    shaped = matrix.reshape(seq_count, length, groups, per_group, HD)
    return shaped.transpose(0, 2, 3, 1, 4).reshape(seq_count * groups, per_group, length, HD)


def from_items(blocks, seq_count):
    count_items, per_group, length, head_size = blocks.shape
    groups = count_items // seq_count
    shaped = blocks.reshape(seq_count, groups, per_group, length, head_size)
    return shaped.transpose(0, 3, 1, 2, 4).reshape(
        seq_count, length, groups * per_group * head_size
    )


def masked_scores(head_q, head_k, q_seg, k_seg, factor):
    scores = jnp.einsum("hqd,hkd->hqk", head_q, head_k, preferred_element_type=jnp.float32) * factor
    matching = q_seg[:, None] == k_seg[None, :]
    return jnp.where(matching[None], scores, NEG)


def body(
    tokens,
    cotangent,
    segment_ids,
    lengths,
    w_query,
    b_query,
    w_key,
    w_value,
    b_value,
    w_attn,
    b_attn,
    ln1_gain,
    ln1_shift,
    w_inner,
    b_inner,
    w_outer,
    b_outer,
    ln2_gain,
    ln2_shift,
):
    shards = (
        w_query,
        b_query,
        w_key,
        w_value,
        b_value,
        w_attn,
        b_attn,
        ln1_gain,
        ln1_shift,
        w_inner,
        b_inner,
        w_outer,
        b_outer,
        ln2_gain,
        ln2_shift,
    )
    seq_count, shard_len, model_width = tokens.shape
    row_count = seq_count * shard_len
    groups = H // math.gcd(H, 4)
    factor = 1.0 / math.sqrt(HD)
    full = (
        lax.all_gather(shards[0], "wt", axis=0, tiled=True),
        lax.all_gather(shards[1], "wt", axis=0, tiled=True),
        lax.all_gather(shards[2], "wt", axis=0, tiled=True),
        lax.all_gather(shards[3], "wt", axis=0, tiled=True),
        lax.all_gather(shards[4], "wt", axis=0, tiled=True),
        lax.all_gather(shards[5], "wt", axis=0, tiled=True),
        lax.all_gather(shards[6], "wt", axis=0, tiled=True),
        lax.all_gather(shards[7], "wt", axis=0, tiled=True),
        lax.all_gather(shards[8], "wt", axis=0, tiled=True),
        lax.all_gather(shards[9], "wt", axis=0, tiled=True),
        lax.all_gather(shards[10], "wt", axis=0, tiled=True),
        lax.all_gather(shards[11], "wt", axis=0, tiled=True),
        lax.all_gather(shards[12], "wt", axis=0, tiled=True),
        lax.all_gather(shards[13], "wt", axis=0, tiled=True),
        lax.all_gather(shards[14], "wt", axis=0, tiled=True),
    )
    rows = tokens.reshape(row_count, model_width)
    query = (product(rows, full[0]) + full[1].astype(jnp.float32)).astype(jnp.bfloat16)
    key_rows = product(rows, full[2]).astype(jnp.bfloat16)
    value_rows = (product(rows, full[3]) + full[4].astype(jnp.float32)).astype(jnp.bfloat16)
    local_kv = (
        key_rows.reshape(seq_count, shard_len, model_width),
        value_rows.reshape(seq_count, shard_len, model_width),
    )
    whole_kv = (
        lax.all_gather(local_kv[0], "ctx", axis=1, tiled=True),
        lax.all_gather(local_kv[1], "ctx", axis=1, tiled=True),
    )
    seq_len = whole_kv[0].shape[1]
    key_segs = jnp.repeat(key_segments(lengths, seq_len), groups, axis=0)
    query_segs = jnp.repeat(segment_ids, groups, axis=0)
    query_items = to_items(query.reshape(seq_count, shard_len, model_width), groups)
    key_items = to_items(whole_kv[0], groups)
    value_items = to_items(whole_kv[1], groups)

    def attend(item):
        head_q, head_k, head_v, q_seg, k_seg = item
        scores = masked_scores(head_q, head_k, q_seg, k_seg, factor)
        highest = jnp.max(scores, axis=-1, keepdims=True)
        totals = jnp.sum(jnp.exp(scores - highest), axis=-1, keepdims=True)
        log_sum = highest + jnp.log(totals)
        probs = jnp.exp(scores - log_sum).astype(jnp.bfloat16)
        mixed = jnp.einsum("hqk,hkd->hqd", probs, head_v, preferred_element_type=jnp.float32)
        return (mixed, log_sum[..., 0])

    attn_items, log_sums = lax.map(
        attend, (query_items, key_items, value_items, query_segs, key_segs)
    )
    attn = from_items(attn_items, seq_count).reshape(row_count, model_width).astype(jnp.bfloat16)
    first_sum = rows.astype(jnp.float32) + product(attn, full[5]) + full[6].astype(jnp.float32)
    hidden, first_pull = jax.vjp(
        norm_rows, first_sum, full[7].astype(jnp.float32), full[8].astype(jnp.float32)
    )
    hidden_low = hidden.astype(jnp.bfloat16)
    inner = product(hidden_low, full[9]) + full[10].astype(jnp.float32)
    active, gelu_pull = jax.vjp(exact_gelu, inner)
    active_low = active.astype(jnp.bfloat16)
    second_sum = hidden + product(active_low, full[11]) + full[12].astype(jnp.float32)
    result, second_pull = jax.vjp(
        norm_rows, second_sum, full[13].astype(jnp.float32), full[14].astype(jnp.float32)
    )
    layer_out = result.astype(jnp.bfloat16).reshape(tokens.shape)
    back = (
        lax.all_gather(shards[0], "wt", axis=0, tiled=True),
        lax.all_gather(shards[1], "wt", axis=0, tiled=True),
        lax.all_gather(shards[2], "wt", axis=0, tiled=True),
        lax.all_gather(shards[3], "wt", axis=0, tiled=True),
        lax.all_gather(shards[4], "wt", axis=0, tiled=True),
        lax.all_gather(shards[5], "wt", axis=0, tiled=True),
        lax.all_gather(shards[6], "wt", axis=0, tiled=True),
        lax.all_gather(shards[7], "wt", axis=0, tiled=True),
        lax.all_gather(shards[8], "wt", axis=0, tiled=True),
        lax.all_gather(shards[9], "wt", axis=0, tiled=True),
        lax.all_gather(shards[10], "wt", axis=0, tiled=True),
        lax.all_gather(shards[11], "wt", axis=0, tiled=True),
        lax.all_gather(shards[12], "wt", axis=0, tiled=True),
        lax.all_gather(shards[13], "wt", axis=0, tiled=True),
        lax.all_gather(shards[14], "wt", axis=0, tiled=True),
    )
    back_kv = (
        lax.all_gather(local_kv[0], "ctx", axis=1, tiled=True),
        lax.all_gather(local_kv[1], "ctx", axis=1, tiled=True),
    )
    back_keys = to_items(back_kv[0], groups)
    back_values = to_items(back_kv[1], groups)
    live = (segment_ids != 0).astype(jnp.float32).reshape(row_count, 1)
    grad_rows = cotangent.reshape(row_count, model_width).astype(jnp.float32) * live
    d_second, d_gain_two, d_shift_two = second_pull(grad_rows)
    d_outer = d_second.astype(jnp.bfloat16)
    g_w_outer = over_rows(active_low, d_outer)
    g_b_outer = jnp.sum(d_outer.astype(jnp.float32), axis=0)
    d_inner = gelu_pull(against(d_outer, back[11]))[0].astype(jnp.bfloat16)
    g_w_inner = over_rows(hidden_low, d_inner)
    g_b_inner = jnp.sum(d_inner.astype(jnp.float32), axis=0)
    d_hidden = d_second + against(d_inner, back[9])
    d_first, d_gain_one, d_shift_one = first_pull(d_hidden)
    d_proj = d_first.astype(jnp.bfloat16)
    g_w_attn = over_rows(attn, d_proj)
    g_b_attn = jnp.sum(d_proj.astype(jnp.float32), axis=0)
    d_attn = against(d_proj, back[5]).astype(jnp.bfloat16)
    d_attn_seq = d_attn.reshape(seq_count, shard_len, model_width)
    d_items = to_items(d_attn_seq, groups)

    def attend_back(item):
        head_q, head_k, head_v, q_seg, k_seg, log_sum, head_d = item
        scores = masked_scores(head_q, head_k, q_seg, k_seg, factor)
        probs = jnp.exp(scores - log_sum[..., None])
        d_probs = jnp.einsum("hqd,hkd->hqk", head_d, head_v, preferred_element_type=jnp.float32)
        center = jnp.sum(probs * d_probs, axis=-1, keepdims=True)
        d_scores = (probs * (d_probs - center)).astype(jnp.bfloat16)
        d_vals = jnp.einsum(
            "hqk,hqd->hkd", probs.astype(jnp.bfloat16), head_d, preferred_element_type=jnp.float32
        )
        d_q = (
            jnp.einsum("hqk,hkd->hqd", d_scores, head_k, preferred_element_type=jnp.float32)
            * factor
        )
        d_k = (
            jnp.einsum("hqk,hqd->hkd", d_scores, head_q, preferred_element_type=jnp.float32)
            * factor
        )
        return (d_q, d_k, d_vals)

    dq_items, dk_items, dv_items = lax.map(
        attend_back, (query_items, back_keys, back_values, query_segs, key_segs, log_sums, d_items)
    )
    d_query = from_items(dq_items, seq_count).reshape(row_count, model_width).astype(jnp.bfloat16)
    partial_kv = (from_items(dk_items, seq_count), from_items(dv_items, seq_count))
    own_kv = (
        lax.psum_scatter(
            partial_kv[0].astype(jnp.bfloat16), "ctx", scatter_dimension=1, tiled=True
        ).astype(jnp.float32),
        lax.psum_scatter(
            partial_kv[1].astype(jnp.bfloat16), "ctx", scatter_dimension=1, tiled=True
        ).astype(jnp.float32),
    )
    d_key = own_kv[0].reshape(row_count, model_width).astype(jnp.bfloat16)
    d_value = own_kv[1].reshape(row_count, model_width).astype(jnp.bfloat16)
    g_w_query = over_rows(rows, d_query)
    g_b_query = jnp.sum(d_query.astype(jnp.float32), axis=0)
    g_w_key = over_rows(rows, d_key)
    g_w_value = over_rows(rows, d_value)
    g_b_value = jnp.sum(d_value.astype(jnp.float32), axis=0)
    input_sum = (
        d_first + against(d_query, back[0]) + against(d_key, back[2]) + against(d_value, back[3])
    )
    grad_input = input_sum.astype(jnp.bfloat16).reshape(tokens.shape)
    grads = (
        g_w_query,
        g_b_query,
        g_w_key,
        g_w_value,
        g_b_value,
        g_w_attn,
        g_b_attn,
        d_gain_one,
        d_shift_one,
        g_w_inner,
        g_b_inner,
        g_w_outer,
        g_b_outer,
        d_gain_two,
        d_shift_two,
    )
    shares = (
        lax.psum_scatter(
            grads[0].astype(jnp.bfloat16), "wt", scatter_dimension=0, tiled=True
        ).astype(jnp.float32),
        lax.psum_scatter(
            grads[1].astype(jnp.bfloat16), "wt", scatter_dimension=0, tiled=True
        ).astype(jnp.float32),
        lax.psum_scatter(
            grads[2].astype(jnp.bfloat16), "wt", scatter_dimension=0, tiled=True
        ).astype(jnp.float32),
        lax.psum_scatter(
            grads[3].astype(jnp.bfloat16), "wt", scatter_dimension=0, tiled=True
        ).astype(jnp.float32),
        lax.psum_scatter(
            grads[4].astype(jnp.bfloat16), "wt", scatter_dimension=0, tiled=True
        ).astype(jnp.float32),
        lax.psum_scatter(
            grads[5].astype(jnp.bfloat16), "wt", scatter_dimension=0, tiled=True
        ).astype(jnp.float32),
        lax.psum_scatter(
            grads[6].astype(jnp.bfloat16), "wt", scatter_dimension=0, tiled=True
        ).astype(jnp.float32),
        lax.psum_scatter(
            grads[7].astype(jnp.bfloat16), "wt", scatter_dimension=0, tiled=True
        ).astype(jnp.float32),
        lax.psum_scatter(
            grads[8].astype(jnp.bfloat16), "wt", scatter_dimension=0, tiled=True
        ).astype(jnp.float32),
        lax.psum_scatter(
            grads[9].astype(jnp.bfloat16), "wt", scatter_dimension=0, tiled=True
        ).astype(jnp.float32),
        lax.psum_scatter(
            grads[10].astype(jnp.bfloat16), "wt", scatter_dimension=0, tiled=True
        ).astype(jnp.float32),
        lax.psum_scatter(
            grads[11].astype(jnp.bfloat16), "wt", scatter_dimension=0, tiled=True
        ).astype(jnp.float32),
        lax.psum_scatter(
            grads[12].astype(jnp.bfloat16), "wt", scatter_dimension=0, tiled=True
        ).astype(jnp.float32),
        lax.psum_scatter(
            grads[13].astype(jnp.bfloat16), "wt", scatter_dimension=0, tiled=True
        ).astype(jnp.float32),
        lax.psum_scatter(
            grads[14].astype(jnp.bfloat16), "wt", scatter_dimension=0, tiled=True
        ).astype(jnp.float32),
    )
    summed = (
        lax.psum(shares[0].astype(jnp.bfloat16), ("seq", "ctx")).astype(jnp.float32),
        lax.psum(shares[1].astype(jnp.bfloat16), ("seq", "ctx")).astype(jnp.float32),
        lax.psum(shares[2].astype(jnp.bfloat16), ("seq", "ctx")).astype(jnp.float32),
        lax.psum(shares[3].astype(jnp.bfloat16), ("seq", "ctx")).astype(jnp.float32),
        lax.psum(shares[4].astype(jnp.bfloat16), ("seq", "ctx")).astype(jnp.float32),
        lax.psum(shares[5].astype(jnp.bfloat16), ("seq", "ctx")).astype(jnp.float32),
        lax.psum(shares[6].astype(jnp.bfloat16), ("seq", "ctx")).astype(jnp.float32),
        lax.psum(shares[7].astype(jnp.bfloat16), ("seq", "ctx")).astype(jnp.float32),
        lax.psum(shares[8].astype(jnp.bfloat16), ("seq", "ctx")).astype(jnp.float32),
        lax.psum(shares[9].astype(jnp.bfloat16), ("seq", "ctx")).astype(jnp.float32),
        lax.psum(shares[10].astype(jnp.bfloat16), ("seq", "ctx")).astype(jnp.float32),
        lax.psum(shares[11].astype(jnp.bfloat16), ("seq", "ctx")).astype(jnp.float32),
        lax.psum(shares[12].astype(jnp.bfloat16), ("seq", "ctx")).astype(jnp.float32),
        lax.psum(shares[13].astype(jnp.bfloat16), ("seq", "ctx")).astype(jnp.float32),
        lax.psum(shares[14].astype(jnp.bfloat16), ("seq", "ctx")).astype(jnp.float32),
    )
    return (layer_out, grad_input) + tuple(summed)


def solution(mesh):
    in_specs = (
        P(("seq", "wt"), "ctx", None),
        P(("seq", "wt"), "ctx", None),
        P(("seq", "wt"), "ctx"),
        P(("seq", "wt"), None),
        P("wt", None),
        P("wt"),
        P("wt", None),
        P("wt", None),
        P("wt"),
        P("wt", None),
        P("wt"),
        P("wt"),
        P("wt"),
        P("wt", None),
        P("wt"),
        P("wt", None),
        P("wt"),
        P("wt"),
        P("wt"),
    )
    out_specs = (
        P(("seq", "wt"), "ctx", None),
        P(("seq", "wt"), "ctx", None),
        P("wt", None),
        P("wt"),
        P("wt", None),
        P("wt", None),
        P("wt"),
        P("wt", None),
        P("wt"),
        P("wt"),
        P("wt"),
        P("wt", None),
        P("wt"),
        P("wt", None),
        P("wt"),
        P("wt"),
        P("wt"),
    )
    return jax.shard_map(body, mesh=mesh, in_specs=in_specs, out_specs=out_specs, check_vma=False)
```

profile of v0, /device:TPU:0, one launch (start us, length us, event | category | flops | bytes accessed | tf_op | source)
XLA Modules:
  0.0 968.8 jit_solution(11220610871833606484)
XLA Ops:
  17.3 21.1 %all-reduce.20 = (bf16[768]{0:T(1024)(128)(2,1)S(1)}, bf16[768]{0:T(1024)(128)(2,1)S(1)}, bf16[768]{0:T(1024)(128)(2,1)S(1)}, bf16[768]{0:T(1024)(128)(2,1)S(1)}...) all-reduce(bf16[768]{0:T(1024)(128)(2,1)S(1)} %dynamic-update-slice, ...), channel_id=1, replica_groups=mesh['seq'=2,'ctx'=4,'wt'=4] {'wt'}, use_global_device_ids=true, to_apply=%add | all-reduce | flops 5376 | bytes 21504
  38.4 4.9 all-gather.16.cloned.1.call-done
  46.9 27.5 %all-gather.12.cloned.1.call-done = bf16[768,768]{1,0:T(8,128)(2,1)} async-done(((bf16[192,768]{1,0:T(8,128)(2,1)}), bf16[768,768]{1,0:T(8,128)(2,1)}) %all-gather.12.cloned.1.call-update) | async-done | bytes 1179664 | tf_op jit(solution)/shard_map/all_gather | solution.py:114
  81.1 13.6 %all-gather = bf16[4,1,768]{2,1,0:T(2,128)(2,1)S(1)} all-gather(bf16[1,1,768]{2,1,0:T(2,128)(2,1)S(1)} %reshape.309), channel_id=1, replica_groups=mesh['seq'=2,'ctx'=4,'wt'=4] {'wt'}, dimensions={0}, use_global_device_ids=true | all-gather | bytes 7680 | tf_op jit(solution)/shard_map/all_gather | solution.py:122
  94.7 11.1 %all-gather.10.cloned.1.call-done = bf16[768,768]{1,0:T(8,128)(2,1)} async-done(((bf16[192,768]{1,0:T(8,128)(2,1)}), bf16[768,768]{1,0:T(8,128)(2,1)}) %all-gather.10.cloned.1.call-update) | async-done | bytes 1179664 | tf_op jit(solution)/shard_map/all_gather | solution.py:112
  108.5 27.4 %all-gather.18.cloned.1.call-done = bf16[2,1024,768]{1,2,0:T(8,128)(2,1)} async-done(((bf16[2,256,768]{1,2,0:T(8,128)(2,1)}), bf16[2,1024,768]{1,2,0:T(8,128)(2,1)}) %all-gather.18.cloned.1.call-update) | async-done | bytes 3145744 | tf_op jit(solution)/shard_map/all_gather | solution.py:138
  135.8 30.9 %all-gather.14.cloned.1.call-done = bf16[2,1024,768]{1,2,0:T(8,128)(2,1)} async-done(((bf16[2,256,768]{1,2,0:T(8,128)(2,1)}), bf16[2,1024,768]{1,2,0:T(8,128)(2,1)}) %all-gather.14.cloned.1.call-update) | async-done | bytes 3145744 | tf_op jit(solution)/shard_map/all_gather | solution.py:137
  166.9 34.3 %while.26 = (s32[]{:T(128)}, bf16[6,4,256,64]{2,3,1,0:T(8,128)(2,1)S(1)}, f32[6,4,256]{2,1,0:T(4,128)S(1)}, s32[6,256]{1,0:T(8,128)S(1)}, s32[6,1024]{1,0:T(8,12...) while((s32[]{:T(128)}, ...), condition=%wide.region_5.6_spmd, body=%wide.region_2.5_spmd.sunk | while | flops 280230912 | bytes 15123561 | solution.py:157
  205.2 83.6 %all-gather.22.cloned.1.call-done = bf16[768,3072]{1,0:T(8,128)(2,1)} async-done(((bf16[192,3072]{1,0:T(8,128)(2,1)}), bf16[768,3072]{1,0:T(8,128)(2,1)}) %all-gather.22.cloned.1.call-update) | async-done | bytes 4718608 | tf_op jit(solution)/shard_map/all_gather | solution.py:121
  288.8 19.8 %multiply_convert_fusion.1 = (bf16[512,3072]{1,0:T(8,128)(2,1)}, f32[512,3072]{1,0:T(8,128)}, f32[512,3072]{1,0:T(8,128)}) fusion(f32[3072]{0:T(1024)S(1)} %bitcast.251, bf16[768,3072]{1,0:T(8,128)(2,1)} %all-gather.22.cloned.1.call-done, f32[512,768]{1,0:T(8,128)S(1)} %get-tuple-element.307, f32[768]{0:T(1024)S(1)} %convert_element_type.289, ...), kind=kOutput, calls=%fused_computation.68 | convolution fusion | flops 2521694208 | bytes 22042624 | tf_op jit(solution)/shard_map/dot_general | solution.py:14
  308.6 69.7 %all-gather.24.cloned.1.call-done = bf16[3072,768]{1,0:T(8,128)(2,1)} async-done(((bf16[768,768]{1,0:T(8,128)(2,1)}), bf16[3072,768]{1,0:T(8,128)(2,1)}) %all-gather.24.cloned.1.call-update) | async-done | bytes 4718608 | tf_op jit(solution)/shard_map/all_gather | solution.py:123
  378.3 6.1 fusion.78
  388.1 7.9 fusion.71
  396.1 3.1 multiply_reduce_fusion.3
  412.5 83.7 %while.27 = (s32[]{:T(128)}, bf16[6,4,256,64]{2,3,1,0:T(8,128)(2,1)}, bf16[6,4,1024,64]{2,3,1,0:T(8,128)(2,1)}, bf16[6,4,1024,64]{2,3,1,0:T(8,128)(2,1)}, s32[6,...) while((s32[]{:T(128)}, ...), condition=%wide.region_16.17_spmd, body=%wide.region_14.16_spmd.sunk | while | flops 687406080 | bytes 37011584 | solution.py:235
  504.4 28.4 %reduce-scatter.17.cloned.1.call-done = bf16[2,256,768]{1,2,0:T(8,128)(2,1)} async-done(((bf16[2,1024,768]{1,2,0:T(8,128)(2,1)}), bf16[2,256,768]{1,2,0:T(8,128)(2,1)}) %reduce-scatter.17.cloned.1.call-update) | async-done | bytes 786448 | tf_op jit(solution)/shard_map/reduce_scatter | solution.py:244
  532.8 3.2 fusion.62
  538.4 34.9 %reduce-scatter.15.cloned.1.call-done = bf16[2,256,768]{1,2,0:T(8,128)(2,1)} async-done(((bf16[2,1024,768]{1,2,0:T(8,128)(2,1)}), bf16[2,256,768]{1,2,0:T(8,128)(2,1)}) %reduce-scatter.15.cloned.1.call-update) | async-done | bytes 786448 | tf_op jit(solution)/shard_map/reduce_scatter | solution.py:241
  573.3 3.2 fusion.61
  578.9 3.2 convolution_convert_fusion.2
  582.3 7.4 convolution_convert_fusion.1
  589.7 6.9 convolution_convert_fusion
  598.3 6.5 reduce-scatter.25.cloned.1.call-done
  606.7 28.2 %reduce-scatter.29.cloned.1.call-done = bf16[192,768]{1,0:T(8,128)(2,1)} async-done(((bf16[768,768]{1,0:T(8,128)(2,1)}), bf16[192,768]{1,0:T(8,128)(2,1)}) %reduce-scatter.29.cloned.1.call-update) | async-done | bytes 294928
  636.8 28.4 %reduce-scatter.27.cloned.1.call-done = bf16[192,768]{1,0:T(8,128)(2,1)} async-done(((bf16[768,768]{1,0:T(8,128)(2,1)}), bf16[192,768]{1,0:T(8,128)(2,1)}) %reduce-scatter.27.cloned.1.call-update) | async-done | bytes 294928
  667.0 28.8 %reduce-scatter.19.cloned.1.call-done = bf16[192,768]{1,0:T(8,128)(2,1)} async-done(((bf16[768,768]{1,0:T(8,128)(2,1)}), bf16[192,768]{1,0:T(8,128)(2,1)}) %reduce-scatter.19.cloned.1.call-update) | async-done | bytes 294928 | tf_op jit(solution)/shard_map/reduce_scatter | solution.py:292
  695.8 86.2 %reduce-scatter.21.cloned.1.call-done = bf16[192,3072]{1,0:T(8,128)(2,1)} async-done(((bf16[768,3072]{1,0:T(8,128)(2,1)}), bf16[192,3072]{1,0:T(8,128)(2,1)}) %reduce-scatter.21.cloned.1.call-update) | async-done | bytes 1179664 | tf_op jit(solution)/shard_map/reduce_scatter | solution.py:304
  782.0 88.0 %reduce-scatter.23.cloned.1.call-done = bf16[768,768]{1,0:T(8,128)(2,1)} async-done(((bf16[3072,768]{1,0:T(8,128)(2,1)}), bf16[768,768]{1,0:T(8,128)(2,1)}) %reduce-scatter.23.cloned.1.call-update) | async-done | bytes 1179664 | tf_op jit(solution)/shard_map/reduce_scatter | solution.py:310
  874.5 3.5 fusion.79
  879.3 18.2 %all-reduce.19 = (bf16[768]{0:T(1024)(128)(2,1)S(1)}, bf16[768]{0:T(1024)(128)(2,1)S(1)}, bf16[768]{0:T(1024)(128)(2,1)S(1)}, bf16[768]{0:T(1024)(128)(2,1)S(1)}...) all-reduce(bf16[768]{0:T(1024)(128)(2,1)S(1)} %dynamic-update-slice, ...), channel_id=1, replica_groups=mesh['seq'=2,'ctx'=4,'wt'=4] {'wt'}, use_global_device_ids=true, to_apply=%add.7 | all-reduce | flops 9984 | bytes 39936
  898.2 12.5 %all-reduce.17 = (bf16[192]{0:T(256)(128)(2,1)S(1)}, bf16[192]{0:T(256)(128)(2,1)S(1)}, bf16[192]{0:T(256)(128)(2,1)S(1)}, bf16[192]{0:T(256)(128)(2,1)S(1)}, bf...) all-reduce(bf16[192]{0:T(256)(128)(2,1)S(1)} %dynamic-slice.9, ...), channel_id=1, replica_groups=mesh['seq'=2,'ctx'=4,'wt'=4] {'seq','ctx'}, use_global_device_ids=true, to_apply=%region_23.24 | all-reduce | flops 2304 | bytes 9216 | tf_op jit(solution)/shard_map/psum | solution.py:325
  926.0 27.6 %all-reduce.23.cloned.1.call-done = (bf16[192,768]{0,1:T(8,128)(2,1)}, bf16[192,768]{0,1:T(8,128)(2,1)}, bf16[192,768]{0,1:T(8,128)(2,1)}, bf16[192,768]{1,0:T(8...) async-done(((bf16[192,768]{0,1:T(8,128)(2,1)}, bf16[192,768]{0,1:T(8,128)(2,1)}, bf16[192,768]{0,1:T(8,128)(2,1)}, bf16[192,768]{1,0:T(8,128)(2,1)}, ...) | async-done | bytes 3538960 | tf_op jit(solution)/shard_map/psum | solution.py:324
  (306 shorter events, 209.6 us)
Async XLA Ops:
  7.2 36.1 %all-gather.16.cloned.1.call-start = ((), (), s32[]{:S(2)}) async-start(), calls=%async_computation.11 | async-start | bytes 1474560 | tf_op jit(solution)/shard_map/all_gather | solution.py:115
  7.9 66.5 %all-gather.12.cloned.1.call-start = ((), (), s32[]{:S(2)}) async-start(), calls=%async_computation.9 | async-start | bytes 1474560 | tf_op jit(solution)/shard_map/all_gather | solution.py:114
  8.7 97.1 %all-gather.10.cloned.1.call-start = ((), (), s32[]{:S(2)}) async-start(), calls=%async_computation.8 | async-start | bytes 1474560 | tf_op jit(solution)/shard_map/all_gather | solution.py:112
  9.4 126.4 %all-gather.18.cloned.1.call-start = ((), (), s32[]{:S(2)}) async-start(), calls=%async_computation.12 | async-start | bytes 3932160 | tf_op jit(solution)/shard_map/all_gather | solution.py:138
  43.3 31.1 %copy-start.21 = (bf16[2,256,768]{2,1,0:T(8,128)(2,1)S(1)}, bf16[2,256,768]{2,1,0:T(8,128)(2,1)}, u32[]{:S(2)}) copy-start(bf16[2,256,768]{2,1,0:T(8,128)(2,1)} %param.23) | copy-start | bytes 2359300
  46.9 119.9 %all-gather.14.cloned.1.call-start = ((), (), s32[]{:S(2)}) async-start(), calls=%async_computation.10 | async-start | bytes 3932160 | tf_op jit(solution)/shard_map/all_gather | solution.py:137
  76.5 3.9 copy-start.16
  76.5 4.6 copy-start.17
  77.7 124.5 %all-gather.20.cloned.1.call-start = ((), (), s32[]{:S(2)}) async-start(), calls=%async_computation.13 | async-start | bytes 1474560 | tf_op jit(solution)/shard_map/all_gather | solution.py:117
  78.3 210.5 %all-gather.22.cloned.1.call-start = ((), (), s32[]{:S(2)}) async-start(), calls=%async_computation.14 | async-start | bytes 5898240 | tf_op jit(solution)/shard_map/all_gather | solution.py:121
  79.1 299.3 %all-gather.24.cloned.1.call-start = ((), (), s32[]{:S(2)}) async-start(), calls=%async_computation.15 | async-start | bytes 5898240 | tf_op jit(solution)/shard_map/all_gather | solution.py:123
  79.8 453.0 %reduce-scatter.17.cloned.1.call-start = ((), (), s32[]{:S(2)}) async-start(), calls=%async_computation.17 | async-start | bytes 3932160 | tf_op jit(solution)/shard_map/reduce_scatter | solution.py:244
  204.9 191.1 %copy-start.2 = (f32[512,768]{1,0:T(8,128)}, f32[512,768]{1,0:T(8,128)S(1)}, u32[]{:S(2)}) copy-start(f32[512,768]{1,0:T(8,128)S(1)} %get-tuple-element.307) | copy-start | bytes 4718596
  378.3 6.4 copy-start.1
  386.2 9.8 %slice-start = ((s8[4718592]{0:T(1024)(128)(4,1)}), s8[4194304]{0:T(1024)(128)(4,1)S(1)}, s32[]{:S(2)}) async-start(s8[4718592]{0:T(1024)(128)(4,1)} %bitcast.253), calls=%async_computation.25 | async-start | bytes 8388608
  386.4 9.6 copy-start.9
  388.1 8.0 slice-start.1
  496.2 77.0 %reduce-scatter.15.cloned.1.call-start = ((), (), s32[]{:S(2)}) async-start(), calls=%async_computation.16 | async-start | bytes 3932160 | tf_op jit(solution)/shard_map/reduce_scatter | solution.py:241
  496.8 108.0 %reduce-scatter.25.cloned.1.call-start = ((), (), s32[]{:S(2)}) async-start(), calls=%async_computation.21 | async-start | bytes 1474560
  504.3 130.6 %reduce-scatter.29.cloned.1.call-start = ((), (), s32[]{:S(2)}) async-start(), calls=%async_computation.23 | async-start | bytes 1474560
  538.3 126.8 %reduce-scatter.27.cloned.1.call-start = ((), (), s32[]{:S(2)}) async-start(), calls=%async_computation.22 | async-start | bytes 1474560
  578.8 117.0 %reduce-scatter.19.cloned.1.call-start = ((), (), s32[]{:S(2)}) async-start(), calls=%async_computation.18 | async-start | bytes 1474560 | tf_op jit(solution)/shard_map/reduce_scatter | solution.py:292
  582.1 199.9 %reduce-scatter.21.cloned.1.call-start = ((), (), s32[]{:S(2)}) async-start(), calls=%async_computation.19 | async-start | bytes 5898240 | tf_op jit(solution)/shard_map/reduce_scatter | solution.py:304
  589.7 280.3 %reduce-scatter.23.cloned.1.call-start = ((), (), s32[]{:S(2)}) async-start(), calls=%async_computation.20 | async-start | bytes 5898240 | tf_op jit(solution)/shard_map/reduce_scatter | solution.py:310
  596.7 273.3 %copy-start.15 = (f32[2,256]{1,0:T(2,128)S(1)}, f32[2,256]{1,0:T(2,128)}, u32[]{:S(2)}) copy-start(f32[2,256]{1,0:T(2,128)} %get-tuple-element.302) | copy-start | bytes 6148
  596.7 356.9 %all-reduce.23.cloned.1.call-start = ((), (), s32[]{:S(2)}) async-start(), calls=%async_computation.24 | async-start | bytes 7667712 | tf_op jit(solution)/shard_map/psum | solution.py:324
  920.3 3.9 copy-start.3
  920.3 3.9 copy-start.4
  920.4 3.9 copy-start.6
  953.6 4.7 copy-start.14
  953.6 5.5 copy-start.13
  956.7 4.4 copy-start.11
  (12 other events, 32.0 us)
Sparse Core Ops, SparseCore 0:
  9.6 33.6 all-gather.15
  44.9 29.5 all-gather.11
  76.0 29.7 all-gather.9
  107.8 28.0 all-gather.17
  137.8 28.9 all-gather.13
  168.2 30.4 all-gather.19
  200.3 88.5 all-gather.21
  290.4 87.8 all-gather.23
  496.3 36.3 reduce-scatter.16
  535.3 37.9 reduce-scatter.14
  575.6 29.1 reduce-scatter.24
  607.0 27.8 reduce-scatter.28
  637.2 27.8 reduce-scatter.26
  667.9 27.8 reduce-scatter.18
  698.0 83.9 reduce-scatter.20
  784.1 85.7 reduce-scatter.22
  874.5 79.0 all-reduce.22
where the time goes:
time: 975 us; the launch traced here: 969 us
  waiting for transfers between devices  617 us (63%)
  matrix products  181 us (19%)
  blocking collectives  65.3 us (7%)
  local copies, waits for them, and re-layouts  47.2 us (5%)
  other arithmetic  40.5 us (4%)
  between operations  16.7 us (2%)
    reduce_scatter x1, waiting for transfers between devices, body(): lax.psum_scatter(grads[11].astype(jnp.bfloat16), 'wt', scatter_dimension=...  88 us
    reduce_scatter x1, waiting for transfers between devices, body(): lax.psum_scatter(grads[9].astype(jnp.bfloat16), 'wt', scatter_dimension=0...  86.2 us
    all_gather x1, waiting for transfers between devices, body(): lax.all_gather(shards[9], 'wt', axis=0, tiled=True)  83.6 us
    all_gather x1, waiting for transfers between devices, body(): lax.all_gather(shards[11], 'wt', axis=0, tiled=True)  69.7 us
    unnamed x20, waiting for transfers between devices  67.8 us
    unnamed x2, blocking collectives  39.3 us
    dot_general x6, matrix products, product(): return jnp.dot(former, latter, preferred_element_type=jnp.float32)  35 us
    reduce_scatter x1, waiting for transfers between devices, body(): lax.psum_scatter(partial_kv[0].astype(jnp.bfloat16), 'ctx', scatter_dimen...  34.9 us
  transfers between devices with their start and end apart: 17, of which 16 were waited for; matrix products, arithmetic and copies ran while one was open for 15% of the time, Pallas kernels for 0%

commit v1 on v0

--- a/solution.py
+++ b/solution.py
@@ -8,6 +8,27 @@
 HD = 64
 NEG = -1000000000.0
 EPS = 1e-05
+
+
+def in_order(blocks, dim):
+    blocks = jnp.moveaxis(blocks, 0, dim)
+    shape = blocks.shape
+    return blocks.reshape(*shape[:dim], shape[dim] * shape[dim + 1], *shape[dim + 2 :])
+
+
+def grow_blocks(shard, axis):
+    size, index = (lax.axis_size(axis), lax.axis_index(axis))
+    parts, distance = (shard[None], 1)
+    while distance < size:
+        other = lax.ppermute(parts, axis, [(i, i ^ distance) for i in range(size)])
+        low = index & distance == 0
+        parts = jnp.concatenate([jnp.where(low, parts, other), jnp.where(low, other, parts)])
+        distance *= 2
+    return parts
+
+
+def collect(x, axis, dim):
+    return in_order(grow_blocks(x, axis), dim)
 
 
 def product(former, latter):
@@ -134,7 +155,7 @@
         value_rows.reshape(seq_count, shard_len, model_width),
     )
     whole_kv = (
-        lax.all_gather(local_kv[0], "ctx", axis=1, tiled=True),
+        collect(local_kv[0], "ctx", 1),
         lax.all_gather(local_kv[1], "ctx", axis=1, tiled=True),
     )
     seq_len = whole_kv[0].shape[1]

time: 975 us -> 946 us (0.970)
  waiting for transfers between devices: 617 us -> 566 us
  local copies, waits for them, and re-layouts: 47.2 us -> 60.1 us
    all_gather x1, waiting for transfers between devices: 30.9 us -> 0.01 us  [body(): lax.all_gather(local_kv[0], 'ctx', axis=1, tiled=True)]
    all_gather x1, waiting for transfers between devices: 27.4 us -> 7.81 us  [body(): lax.all_gather(local_kv[1], 'ctx', axis=1, tiled=True)]
    unnamed x93 -> x95, local copies, waits for them, and re-layouts: 27.9 us -> 28.2 us
  transfers between devices with their start and end apart: 17 -> 19, of which waited for: 16 -> 17; matrix products, arithmetic and copies ran while one was open for 15% -> 20% of each run, Pallas kernels for 0% -> 0%
where the time goes in v1:
time: 946 us; the launch traced here: 939 us
  waiting for transfers between devices  566 us (60%)
  matrix products  184 us (19%)
  blocking collectives  65 us (7%)
  local copies, waits for them, and re-layouts  60.1 us (6%)
  other arithmetic  43.8 us (5%)
  between operations  16.8 us (2%)
    reduce_scatter x1, waiting for transfers between devices, body(): lax.psum_scatter(grads[9].astype(jnp.bfloat16), 'wt', scatter_dimension=0...  88 us
    reduce_scatter x1, waiting for transfers between devices, body(): lax.psum_scatter(grads[11].astype(jnp.bfloat16), 'wt', scatter_dimension=...  86.2 us
    all_gather x1, waiting for transfers between devices, body(): lax.all_gather(shards[9], 'wt', axis=0, tiled=True)  78.5 us
    all_gather x1, waiting for transfers between devices, body(): lax.all_gather(shards[11], 'wt', axis=0, tiled=True)  69.6 us
    unnamed x20, waiting for transfers between devices  67.6 us
    unnamed x2, blocking collectives  39.3 us
    dot_general x6, matrix products, product(): return jnp.dot(former, latter, preferred_element_type=jnp.float32)  35.1 us
    reduce_scatter x1, waiting for transfers between devices, body(): lax.psum_scatter(partial_kv[1].astype(jnp.bfloat16), 'ctx', scatter_dimen...  34.9 us
  transfers between devices with their start and end apart: 19, of which 17 were waited for; matrix products, arithmetic and copies ran while one was open for 20% of the time, Pallas kernels for 0%

profile of v1, /device:TPU:0, one launch (start us, length us, event | category | flops | bytes accessed | tf_op | source)
XLA Modules:
  0.0 938.6 jit_solution(15649347077492127749)
XLA Ops:
  17.3 21.1 %all-reduce.20 = (bf16[768]{0:T(1024)(128)(2,1)S(1)}, bf16[768]{0:T(1024)(128)(2,1)S(1)}, bf16[768]{0:T(1024)(128)(2,1)S(1)}, bf16[768]{0:T(1024)(128)(2,1)S(1)}...) all-reduce(bf16[768]{0:T(1024)(128)(2,1)S(1)} %dynamic-update-slice, ...), channel_id=1, replica_groups=mesh['seq'=2,'ctx'=4,'wt'=4] {'wt'}, use_global_device_ids=true, to_apply=%add | all-reduce | flops 5376 | bytes 21504
  38.4 4.9 all-gather.14.cloned.1.call-done
  48.7 25.7 %all-gather.12.cloned.1.call-done = bf16[768,768]{1,0:T(8,128)(2,1)} async-done(((bf16[192,768]{1,0:T(8,128)(2,1)}), bf16[768,768]{1,0:T(8,128)(2,1)}) %all-gather.12.cloned.1.call-update) | async-done | bytes 1179664 | tf_op jit(solution)/shard_map/all_gather | solution.py:135
  82.4 13.3 %all-gather = bf16[4,1,768]{2,1,0:T(2,128)(2,1)S(1)} all-gather(bf16[1,1,768]{2,1,0:T(2,128)(2,1)S(1)} %reshape.311), channel_id=1, replica_groups=mesh['seq'=2,'ctx'=4,'wt'=4] {'wt'}, dimensions={0}, use_global_device_ids=true | all-gather | bytes 7680 | tf_op jit(solution)/shard_map/all_gather | solution.py:143
  96.3 9.5 %all-gather.10.cloned.1.call-done = bf16[768,768]{1,0:T(8,128)(2,1)} async-done(((bf16[192,768]{1,0:T(8,128)(2,1)}), bf16[768,768]{1,0:T(8,128)(2,1)}) %all-gather.10.cloned.1.call-update) | async-done | bytes 1179664 | tf_op jit(solution)/shard_map/all_gather | solution.py:133
  112.2 5.6 collective-permute-done.1
  119.7 3.7 copy.91
  123.3 4.7 reshape_reshape.12
  128.0 7.8 all-gather.16.cloned.1.call-done
  136.8 37.2 %while.26 = (s32[]{:T(128)}, bf16[6,4,256,64]{2,3,1,0:T(8,128)(2,1)}, f32[6,4,256]{2,1,0:T(4,128)S(1)}, s32[6,256]{1,0:T(8,128)S(1)}, s32[6,1024]{1,0:T(8,128)S(...) while((s32[]{:T(128)}, ...), condition=%wide.region_5.6_spmd, body=%wide.region_2.5_spmd.sunk | while | flops 280230912 | bytes 15123561 | solution.py:178
  179.2 78.5 %all-gather.20.cloned.1.call-done = bf16[768,3072]{1,0:T(8,128)(2,1)} async-done(((bf16[192,3072]{1,0:T(8,128)(2,1)}), bf16[768,3072]{1,0:T(8,128)(2,1)}) %all-gather.20.cloned.1.call-update) | async-done | bytes 4718608 | tf_op jit(solution)/shard_map/all_gather | solution.py:142
  257.7 19.8 %multiply_convert_fusion.1 = (bf16[512,3072]{1,0:T(8,128)(2,1)}, f32[512,3072]{1,0:T(8,128)}, f32[512,3072]{1,0:T(8,128)}) fusion(f32[3072]{0:T(1024)S(1)} %bitcast.262, bf16[768,3072]{1,0:T(8,128)(2,1)} %all-gather.20.cloned.1.call-done, f32[512,768]{1,0:T(8,128)S(1)} %get-tuple-element.311, f32[768]{0:T(1024)S(1)} %convert_element_type.289, ...), kind=kOutput, calls=%fused_computation.68 | convolution fusion | flops 2521694208 | bytes 22042624 | tf_op jit(solution)/shard_map/dot_general | solution.py:35
  277.6 69.6 %all-gather.22.cloned.1.call-done = bf16[3072,768]{1,0:T(8,128)(2,1)} async-done(((bf16[768,768]{1,0:T(8,128)(2,1)}), bf16[3072,768]{1,0:T(8,128)(2,1)}) %all-gather.22.cloned.1.call-update) | async-done | bytes 4718608 | tf_op jit(solution)/shard_map/all_gather | solution.py:144
  347.2 6.1 fusion.78
  357.3 8.1 fusion.71
  381.9 83.7 %while.27 = (s32[]{:T(128)}, bf16[6,4,256,64]{2,3,1,0:T(8,128)(2,1)}, bf16[6,4,1024,64]{2,3,1,0:T(8,128)(2,1)}, bf16[6,4,1024,64]{2,3,1,0:T(8,128)(2,1)}, s32[6,...) while((s32[]{:T(128)}, ...), condition=%wide.region_16.17_spmd, body=%wide.region_14.16_spmd.sunk | while | flops 687406080 | bytes 37011584 | solution.py:256
  473.8 28.7 %reduce-scatter.15.cloned.1.call-done = bf16[2,256,768]{1,2,0:T(8,128)(2,1)} async-done(((bf16[2,1024,768]{1,2,0:T(8,128)(2,1)}), bf16[2,256,768]{1,2,0:T(8,128)(2,1)}) %reduce-scatter.15.cloned.1.call-update) | async-done | bytes 786448 | tf_op jit(solution)/shard_map/reduce_scatter | solution.py:262
  502.5 3.2 fusion.61
  508.1 34.9 %reduce-scatter.17.cloned.1.call-done = bf16[2,256,768]{1,2,0:T(8,128)(2,1)} async-done(((bf16[2,1024,768]{1,2,0:T(8,128)(2,1)}), bf16[2,256,768]{1,2,0:T(8,128)(2,1)}) %reduce-scatter.17.cloned.1.call-update) | async-done | bytes 786448 | tf_op jit(solution)/shard_map/reduce_scatter | solution.py:265
  548.6 3.2 convolution_convert_fusion.2
  552.0 6.9 convolution_convert_fusion
  559.0 7.4 convolution_convert_fusion.1
  568.1 6.5 reduce-scatter.25.cloned.1.call-done
  576.5 28.2 %reduce-scatter.27.cloned.1.call-done = bf16[192,768]{1,0:T(8,128)(2,1)} async-done(((bf16[768,768]{1,0:T(8,128)(2,1)}), bf16[192,768]{1,0:T(8,128)(2,1)}) %reduce-scatter.27.cloned.1.call-update) | async-done | bytes 294928
  606.5 28.4 %reduce-scatter.29.cloned.1.call-done = bf16[192,768]{1,0:T(8,128)(2,1)} async-done(((bf16[768,768]{1,0:T(8,128)(2,1)}), bf16[192,768]{1,0:T(8,128)(2,1)}) %reduce-scatter.29.cloned.1.call-update) | async-done | bytes 294928
  636.8 28.8 %reduce-scatter.19.cloned.1.call-done = bf16[192,768]{1,0:T(8,128)(2,1)} async-done(((bf16[768,768]{1,0:T(8,128)(2,1)}), bf16[192,768]{1,0:T(8,128)(2,1)}) %reduce-scatter.19.cloned.1.call-update) | async-done | bytes 294928 | tf_op jit(solution)/shard_map/reduce_scatter | solution.py:313
  665.6 86.2 %reduce-scatter.23.cloned.1.call-done = bf16[768,768]{1,0:T(8,128)(2,1)} async-done(((bf16[3072,768]{1,0:T(8,128)(2,1)}), bf16[768,768]{1,0:T(8,128)(2,1)}) %reduce-scatter.23.cloned.1.call-update) | async-done | bytes 1179664 | tf_op jit(solution)/shard_map/reduce_scatter | solution.py:331
  751.7 88.0 %reduce-scatter.21.cloned.1.call-done = bf16[192,3072]{1,0:T(8,128)(2,1)} async-done(((bf16[768,3072]{1,0:T(8,128)(2,1)}), bf16[192,3072]{1,0:T(8,128)(2,1)}) %reduce-scatter.21.cloned.1.call-update) | async-done | bytes 1179664 | tf_op jit(solution)/shard_map/reduce_scatter | solution.py:325
  844.3 3.5 fusion.79
  849.1 18.2 %all-reduce.19 = (bf16[768]{0:T(1024)(128)(2,1)S(1)}, bf16[768]{0:T(1024)(128)(2,1)S(1)}, bf16[768]{0:T(1024)(128)(2,1)S(1)}, bf16[768]{0:T(1024)(128)(2,1)S(1)}...) all-reduce(bf16[768]{0:T(1024)(128)(2,1)S(1)} %dynamic-update-slice, ...), channel_id=1, replica_groups=mesh['seq'=2,'ctx'=4,'wt'=4] {'wt'}, use_global_device_ids=true, to_apply=%add.7 | all-reduce | flops 9984 | bytes 39936
  867.9 12.5 %all-reduce.17 = (bf16[192]{0:T(256)(128)(2,1)S(1)}, bf16[192]{0:T(256)(128)(2,1)S(1)}, bf16[192]{0:T(256)(128)(2,1)S(1)}, bf16[192]{0:T(256)(128)(2,1)S(1)}, bf...) all-reduce(bf16[192]{0:T(256)(128)(2,1)S(1)} %dynamic-slice.9, ...), channel_id=1, replica_groups=mesh['seq'=2,'ctx'=4,'wt'=4] {'seq','ctx'}, use_global_device_ids=true, to_apply=%region_23.24 | all-reduce | flops 2304 | bytes 9216 | tf_op jit(solution)/shard_map/psum | solution.py:346
  895.8 27.6 %all-reduce.23.cloned.1.call-done = (bf16[192,768]{0,1:T(8,128)(2,1)}, bf16[192,768]{0,1:T(8,128)(2,1)}, bf16[192,768]{0,1:T(8,128)(2,1)}, bf16[192,768]{1,0:T(8...) async-done(((bf16[192,768]{0,1:T(8,128)(2,1)}, bf16[192,768]{0,1:T(8,128)(2,1)}, bf16[192,768]{0,1:T(8,128)(2,1)}, bf16[192,768]{1,0:T(8,128)(2,1)}, ...) | async-done | bytes 3538960 | tf_op jit(solution)/shard_map/psum | solution.py:345
  (318 shorter events, 230.8 us)
Async XLA Ops:
  7.2 36.1 %all-gather.14.cloned.1.call-start = ((), (), s32[]{:S(2)}) async-start(), calls=%async_computation.10 | async-start | bytes 1474560 | tf_op jit(solution)/shard_map/all_gather | solution.py:136
  7.9 66.5 %all-gather.12.cloned.1.call-start = ((), (), s32[]{:S(2)}) async-start(), calls=%async_computation.9 | async-start | bytes 1474560 | tf_op jit(solution)/shard_map/all_gather | solution.py:135
  8.7 97.2 %all-gather.10.cloned.1.call-start = ((), (), s32[]{:S(2)}) async-start(), calls=%async_computation.8 | async-start | bytes 1474560 | tf_op jit(solution)/shard_map/all_gather | solution.py:133
  9.4 126.4 %all-gather.16.cloned.1.call-start = ((), (), s32[]{:S(2)}) async-start(), calls=%async_computation.11 | async-start | bytes 3932160 | tf_op jit(solution)/shard_map/all_gather | solution.py:159
  45.6 28.9 %copy-start.21 = (bf16[2,256,768]{2,1,0:T(8,128)(2,1)S(1)}, bf16[2,256,768]{2,1,0:T(8,128)(2,1)}, u32[]{:S(2)}) copy-start(bf16[2,256,768]{2,1,0:T(8,128)(2,1)} %param.23) | copy-start | bytes 2359300
  46.8 129.6 %all-gather.18.cloned.1.call-start = ((), (), s32[]{:S(2)}) async-start(), calls=%async_computation.12 | async-start | bytes 1474560 | tf_op jit(solution)/shard_map/all_gather | solution.py:138
  47.4 210.3 %all-gather.20.cloned.1.call-start = ((), (), s32[]{:S(2)}) async-start(), calls=%async_computation.13 | async-start | bytes 5898240 | tf_op jit(solution)/shard_map/all_gather | solution.py:142
  48.0 299.2 %all-gather.22.cloned.1.call-start = ((), (), s32[]{:S(2)}) async-start(), calls=%async_computation.14 | async-start | bytes 5898240 | tf_op jit(solution)/shard_map/all_gather | solution.py:144
  48.7 332.3 %all-gather.24.cloned.1.call-start = ((), (), s32[]{:S(2)}) async-start(), calls=%async_computation.15 | async-start | bytes 3932160 | tf_op jit(solution)/shard_map/all_gather | solution.py:213
  76.5 2.4 collective-permute-start
  76.6 5.1 copy-start.18
  76.6 5.7 copy-start.16
  76.6 5.8 copy-start.17
  80.3 37.5 %collective-permute-start.1 = (bf16[2,2,256,768]{3,2,1,0:T(8,128)(2,1)}, bf16[2,2,256,768]{3,2,1,0:T(8,128)(2,1)}, u32[]{:S(2)}, u32[]{:S(2)}) collective-permute-start(bf16[2,2,256,768]{3,2,1,0:T(8,128)(2,1)} %pad_maximum_fusion), channel_id=1, source_target_pairs={{0,8},{4,12},{8,0},{12,4},{1,9},{5,13},{9,1},{13,5},{2,10},{6,14},... | collective-permute-start | bytes 4718600 | tf_op jit(solution)/shard_map/ppermute | solution.py:23
  112.0 390.6 %reduce-scatter.15.cloned.1.call-start = ((), (), s32[]{:S(2)}) async-start(), calls=%async_computation.16 | async-start | bytes 3932160 | tf_op jit(solution)/shard_map/reduce_scatter | solution.py:262
  178.9 186.5 %copy-start.1 = (f32[512,768]{1,0:T(8,128)}, f32[512,768]{1,0:T(8,128)S(1)}, u32[]{:S(2)}) copy-start(f32[512,768]{1,0:T(8,128)S(1)} %get-tuple-element.311) | copy-start | bytes 4718596
  347.2 6.4 copy-start
  355.1 10.3 %slice-start = ((s8[4718592]{0:T(1024)(128)(4,1)}), s8[4194304]{0:T(1024)(128)(4,1)S(1)}, s32[]{:S(2)}) async-start(s8[4718592]{0:T(1024)(128)(4,1)} %bitcast.264), calls=%async_computation.25 | async-start | bytes 8388608
  355.3 10.1 %copy-start.9 = (bf16[512,768]{1,0:T(8,128)(2,1)}, bf16[512,768]{1,0:T(8,128)(2,1)S(1)}, u32[]{:S(2)}) copy-start(bf16[512,768]{1,0:T(8,128)(2,1)S(1)} %get-tuple-element.287) | copy-start | bytes 2359300
  357.3 8.1 slice-start.1
  465.6 77.4 %reduce-scatter.17.cloned.1.call-start = ((), (), s32[]{:S(2)}) async-start(), calls=%async_computation.17 | async-start | bytes 3932160 | tf_op jit(solution)/shard_map/reduce_scatter | solution.py:265
  466.2 108.4 %reduce-scatter.25.cloned.1.call-start = ((), (), s32[]{:S(2)}) async-start(), calls=%async_computation.21 | async-start | bytes 1474560
  473.7 130.9 %reduce-scatter.27.cloned.1.call-start = ((), (), s32[]{:S(2)}) async-start(), calls=%async_computation.22 | async-start | bytes 1474560
  508.1 126.8 %reduce-scatter.29.cloned.1.call-start = ((), (), s32[]{:S(2)}) async-start(), calls=%async_computation.23 | async-start | bytes 1474560
  548.6 117.0 %reduce-scatter.19.cloned.1.call-start = ((), (), s32[]{:S(2)}) async-start(), calls=%async_computation.18 | async-start | bytes 1474560 | tf_op jit(solution)/shard_map/reduce_scatter | solution.py:313
  551.8 199.9 %reduce-scatter.23.cloned.1.call-start = ((), (), s32[]{:S(2)}) async-start(), calls=%async_computation.20 | async-start | bytes 5898240 | tf_op jit(solution)/shard_map/reduce_scatter | solution.py:331
  558.9 280.8 %reduce-scatter.21.cloned.1.call-start = ((), (), s32[]{:S(2)}) async-start(), calls=%async_computation.19 | async-start | bytes 5898240 | tf_op jit(solution)/shard_map/reduce_scatter | solution.py:325
  566.4 273.3 %copy-start.15 = (f32[2,256]{1,0:T(2,128)S(1)}, f32[2,256]{1,0:T(2,128)}, u32[]{:S(2)}) copy-start(f32[2,256]{1,0:T(2,128)} %get-tuple-element.306) | copy-start | bytes 6148
  566.4 356.9 %all-reduce.23.cloned.1.call-start = ((), (), s32[]{:S(2)}) async-start(), calls=%async_computation.24 | async-start | bytes 7667712 | tf_op jit(solution)/shard_map/psum | solution.py:345
  923.4 4.7 copy-start.14
  923.4 5.5 copy-start.13
  926.5 4.4 copy-start.11
  (15 other events, 42.8 us)
Sparse Core Ops, SparseCore 0:
  9.6 33.6 all-gather.13
  44.9 29.5 all-gather.11
  76.0 29.7 all-gather.9
  107.8 27.9 all-gather.15
  137.3 30.4 all-gather.17
  169.2 88.5 all-gather.19
  259.3 87.8 all-gather.21
  348.7 27.3 all-gather.23
  465.7 36.7 reduce-scatter.14
  505.1 37.9 reduce-scatter.16
  545.3 29.1 reduce-scatter.24
  576.7 27.8 reduce-scatter.26
  607.0 27.8 reduce-scatter.28
  637.6 27.8 reduce-scatter.18
  667.7 83.9 reduce-scatter.22
  753.9 85.7 reduce-scatter.20
  844.3 79.0 all-reduce.22
